TPU v7x, 128 devices: a whole 4x4x4 slice. The times are simulated.
128 devices in a mesh: fsdp: 64 (over x, z, y_hi, core), mat: 2 (over y_lo).
Axes of the slice: x: 4, y: 4 (y_hi: 2, y_lo: 2; y = y_hi * 2 + y_lo), z: 4, core: 2. Of those that a mesh axis runs over, the one named last changes fastest.
Arguments:
- gradient: bfloat16 [8192, 14336], P('fsdp', 'mat'), may hold values from -40000 to 40000, as said below
- weight: bfloat16 [8192, 14336], P('fsdp', 'mat'), may hold values from -6 to 6
- projector: bfloat16 [8192, 768], P('fsdp'), may hold values from -0.0625 to 0.0625
- first_moment: float32 [768, 14336], P('fsdp', 'mat'), may hold values from -6 to 6
- second_moment: float32 [768, 14336], P('fsdp', 'mat'), may hold values from 0.25 to 4
Outputs:
- new_weight: bfloat16 [8192, 14336], P('fsdp', 'mat')
- new_first: float32 [768, 14336], P('fsdp', 'mat')
- new_second: float32 [768, 14336], P('fsdp', 'mat')
Inputs may be any that keep to these rules, and one draw needn't show every extreme that they name: gradient entries are finite and not all zero.
All inputs are finite; a program needn't handle non-finite values.
Results may differ from a plain program's by a relative error of at most 0.0017.
Values may be sent and summed in bfloat16 or wider, within the bound.
A program may use at most 128 MiB of HBM per device.

v0:
```python
import jax
import jax.numpy as jnp
from jax import lax
from jax.sharding import PartitionSpec as P

D = 8192
FW = 14336


def adam_moments(low, clip, first_moment, second_moment):
    scaled = clip * low
    new_first = 0.9 * first_moment + 0.1 * scaled
    new_second = 0.95 * second_moment + 0.05 * scaled * scaled
    direction = (new_first / (jnp.sqrt(new_second) + 1e-08)).astype(jnp.bfloat16)
    return (new_first, new_second, direction)


def shards(gradient, weight, projector, first_moment, second_moment):
    wide = gradient.astype(jnp.float32)
    squares = lax.psum(jnp.sum(wide * wide), ("fsdp", "mat"))
    clip = jnp.minimum(1.0, 1.0 / jnp.sqrt(squares / (D * FW) + 1e-06))
    grad_cols, weight_cols = (
        lax.all_to_all(gradient, "fsdp", split_axis=1, concat_axis=0, tiled=True),
        lax.all_to_all(weight, "fsdp", split_axis=1, concat_axis=0, tiled=True),
    )
    whole_projector = lax.all_gather(projector, "fsdp", axis=0, tiled=True)
    first_cols, second_cols = (
        lax.all_to_all(first_moment, "fsdp", split_axis=1, concat_axis=0, tiled=True),
        lax.all_to_all(second_moment, "fsdp", split_axis=1, concat_axis=0, tiled=True),
    )
    low = lax.dot_general(
        whole_projector, grad_cols, (((0,), (0,)), ((), ())), preferred_element_type=jnp.float32
    )
    first_next, second_next, direction = adam_moments(low, clip, first_cols, second_cols)
    update = jnp.dot(whole_projector, direction, preferred_element_type=jnp.float32)
    weight_next = (weight_cols.astype(jnp.float32) - 0.25 * update).astype(jnp.bfloat16)
    new_first, new_second = (
        lax.all_to_all(first_next, "fsdp", split_axis=0, concat_axis=1, tiled=True),
        lax.all_to_all(second_next, "fsdp", split_axis=0, concat_axis=1, tiled=True),
    )
    new_weight = lax.all_to_all(weight_next, "fsdp", split_axis=0, concat_axis=1, tiled=True)
    return (new_weight, new_first, new_second)


def solution(mesh):
    return jax.shard_map(
        shards,
        mesh=mesh,
        in_specs=(
            P("fsdp", "mat"),
            P("fsdp", "mat"),
            P("fsdp", None),
            P("fsdp", "mat"),
            P("fsdp", "mat"),
        ),
        out_specs=(P("fsdp", "mat"), P("fsdp", "mat"), P("fsdp", "mat")),
        check_vma=False,
    )
```

profile of v0, /device:TPU:1, one launch (start us, length us, event | category | flops | bytes accessed | tf_op | source)
XLA Modules:
  0.0 277.6 jit_solution(10250345622244978523)
XLA Ops:
  7.2 0.7 all-gather.2.cloned.1.call-update
  7.9 1.2 all_to_all.88
  9.2 1.0 copy.28
  10.2 12.6 %all-to-all-start.1 = ((f32[12,64,112]{2,0,1:T(8,128)}), f32[12,64,112]{2,0,1:T(8,128)S(1)}, u32[]{:S(2)}, u32[]{:S(2)}) async-start(f32[12,64,112]{2,0,1:T(8,128)} %copy.28), calls=%async_computation.1 | async-start | bytes 1048576 | tf_op jit(solution)/shard_map/all_to_all | solution.py:28
  23.0 1.1 copy.32
  24.1 13.7 %all-to-all-done.1 = f32[12,64,112]{2,0,1:T(8,128)S(1)} async-done(((f32[12,64,112]{2,0,1:T(8,128)}), f32[12,64,112]{2,0,1:T(8,128)S(1)}, u32[]{:S(2)}, u32[]{:S(2)}) %all-to-all-start.1) | async-done | bytes 344096 | tf_op jit(solution)/shard_map/all_to_all | solution.py:28
  37.8 4.6 %all-to-all-start.3 = ((f32[12,64,112]{2,0,1:T(8,128)}), f32[12,64,112]{2,0,1:T(8,128)S(1)}, u32[]{:S(2)}, u32[]{:S(2)}) async-start(f32[12,64,112]{2,0,1:T(8,128)} %copy.32), calls=%async_computation.3 | async-start | bytes 1048576 | tf_op jit(solution)/shard_map/all_to_all | solution.py:29
  42.4 2.3 copy.29
  44.7 12.2 %all-to-all-done.3 = f32[12,64,112]{2,0,1:T(8,128)S(1)} async-done(((f32[12,64,112]{2,0,1:T(8,128)}), f32[12,64,112]{2,0,1:T(8,128)S(1)}, u32[]{:S(2)}, u32[]{:S(2)}) %all-to-all-start.3) | async-done | bytes 344096 | tf_op jit(solution)/shard_map/all_to_all | solution.py:29
  56.9 4.6 %all-to-all-start.2 = ((bf16[128,64,112]{0,2,1:T(8,128)(2,1)}), bf16[128,64,112]{0,2,1:T(8,128)(2,1)S(1)}, u32[]{:S(2)}, u32[]{:S(2)}) async-start(bf16[128,64,112]{0,2,1:T(8,128)(2,1)} %bitcast.48), calls=%async_computation.2 | async-start | bytes 3670016 | tf_op jit(solution)/shard_map/all_to_all | solution.py:23
  61.5 3.9 %copy.26 = bf16[128,7168]{0,1:T(8,128)(2,1)} copy(bf16[128,7168]{1,0:T(8,128)(2,1)} %param.6) | data formatting | bytes 3670016 | tf_op args[1]
  65.4 26.3 %all-to-all-done.2 = bf16[128,64,112]{0,2,1:T(8,128)(2,1)S(1)} async-done(((bf16[128,64,112]{0,2,1:T(8,128)(2,1)}), bf16[128,64,112]{0,2,1:T(8,128)(2,1)S(1)}, u32[]{:S(2)}, u32[]{:S(2)}) %all-to-all-start.2) | async-done | bytes 1835040 | tf_op jit(solution)/shard_map/all_to_all | solution.py:23
  91.7 8.5 %all-to-all-start = ((bf16[128,64,112]{0,2,1:T(8,128)(2,1)}), bf16[128,64,112]{0,2,1:T(8,128)(2,1)}, u32[]{:S(2)}, u32[]{:S(2)}) async-start(bf16[128,64,112]{0,2,1:T(8,128)(2,1)} %bitcast.46), calls=%async_computation | async-start | bytes 3670016 | tf_op jit(solution)/shard_map/all_to_all | solution.py:24
  100.2 3.0 %multiply_reduce_fusion = f32[]{:T(128)} fusion(bf16[128,7168]{1,0:T(8,128)(2,1)} %param.5), kind=kLoop, calls=%fused_computation.5 | loop fusion | flops 2752511 | bytes 1835012 | tf_op jit(solution)/shard_map/reduce_sum | solution.py:20
  103.2 79.7 %psum.7 = f32[]{:T(128)} all-reduce(f32[]{:T(128)} %multiply_reduce_fusion), channel_id=1, replica_groups=mesh['fsdp'=64,'mat'=2] {'fsdp','mat'}, use_global_device_ids=true, to_apply=%region_1.0 | all-reduce | flops 1 | bytes 8 | tf_op jit(solution)/shard_map/psum | solution.py:20
  183.7 0.9 copy.31
  184.9 0.7 copy-done.3
  185.7 6.5 %fusion.10 = (f32[768,112]{0,1:T(8,128)S(1)}, f32[768,112]{0,1:T(8,128)S(1)}) fusion(f32[768,112]{0,1:T(8,128)S(1)} %copy.33, f32[768,112]{0,1:T(8,128)S(1)} %copy-done.3, bf16[8192,768]{1,0:T(8,128)(2,1)} %all-gather.2.cloned.1.call-done, f32[]{:T(128)S(6)} %min.3, bf16[128,64,112]{0,2,1:T(8,128)(2,1)S(1)} %all-to-all-done.2), kind=kOutput, calls=%fused_computation.15 | convolution fusion | flops 1409802240 | bytes 15794180 | tf_op jit(solution)/shard_map/dot_general | solution.py:31
  192.4 0.8 all_to_all.100
  193.2 6.5 %all-to-all-start.5 = ((f32[64,12,112]{2,1,0:T(8,128)}), f32[64,12,112]{2,1,0:T(8,128)S(1)}, u32[]{:S(2)}, u32[]{:S(2)}) async-start(f32[64,12,112]{2,1,0:T(8,128)} %all_to_all.100), calls=%async_computation.5 | async-start | bytes 1048576 | tf_op jit(solution)/shard_map/all_to_all | solution.py:38
  199.9 0.9 all_to_all.104
  200.8 12.9 %all-to-all-done.5 = f32[64,12,112]{2,1,0:T(8,128)S(1)} async-done(((f32[64,12,112]{2,1,0:T(8,128)}), f32[64,12,112]{2,1,0:T(8,128)S(1)}, u32[]{:S(2)}, u32[]{:S(2)}) %all-to-all-start.5) | async-done | bytes 344096 | tf_op jit(solution)/shard_map/all_to_all | solution.py:38
  213.7 4.6 %all-to-all-start.6 = ((f32[64,12,112]{2,1,0:T(8,128)}), f32[64,12,112]{2,1,0:T(8,128)S(1)}, u32[]{:S(2)}, u32[]{:S(2)}) async-start(f32[64,12,112]{2,1,0:T(8,128)} %all_to_all.104), calls=%async_computation.6 | async-start | bytes 1048576 | tf_op jit(solution)/shard_map/all_to_all | solution.py:39
  218.3 9.1 %fusion.6 = bf16[14,64,8,128]{3,2,1,0:T(8,128)(2,1)S(1)} fusion(bf16[8192,768]{1,0:T(8,128)(2,1)} %all-gather.2.cloned.1.call-done, f32[768,112]{0,1:T(8,128)S(1)} %get-tuple-element.10, f32[768,112]{0,1:T(8,128)S(1)} %get-tuple-element.9, bf16[128,64,112]{0,2,1:T(8,128)(2,1)} %all-to-all-done), kind=kOutput, calls=%fused_computation.10 | convolution fusion | flops 1413214208 | bytes 16941056 | tf_op jit(solution)/shard_map/dot_general | solution.py:35
  227.4 1.5 copy.55
  229.0 3.4 %all-to-all-done.6 = f32[64,12,112]{2,1,0:T(8,128)S(1)} async-done(((f32[64,12,112]{2,1,0:T(8,128)}), f32[64,12,112]{2,1,0:T(8,128)S(1)}, u32[]{:S(2)}, u32[]{:S(2)}) %all-to-all-start.6) | async-done | bytes 344096 | tf_op jit(solution)/shard_map/all_to_all | solution.py:39
  232.3 0.8 copy-done.1
  233.1 7.0 %all-to-all-start.4 = ((bf16[64,128,112]{1,2,0:T(8,128)(2,1)}), bf16[64,128,112]{1,2,0:T(8,128)(2,1)S(1)}, u32[]{:S(2)}, u32[]{:S(2)}) async-start(bf16[64,128,112]{1,2,0:T(8,128)(2,1)} %bitcast.45), calls=%async_computation.4 | async-start | bytes 3670016 | tf_op jit(solution)/shard_map/all_to_all | solution.py:41
  240.3 1.0 all_to_all.103
  241.5 1.0 all_to_all.107
  242.6 25.4 %all-to-all-done.4 = bf16[64,128,112]{1,2,0:T(8,128)(2,1)S(1)} async-done(((bf16[64,128,112]{1,2,0:T(8,128)(2,1)}), bf16[64,128,112]{1,2,0:T(8,128)(2,1)S(1)}, u32[]{:S(2)}, u32[]{:S(2)}) %all-to-all-start.4) | async-done | bytes 1835040 | tf_op jit(solution)/shard_map/all_to_all | solution.py:41
  267.9 2.9 %copy.39 = bf16[128,7168]{1,0:T(8,128)(2,1)} copy(bf16[128,7168]{0,1:T(8,128)(2,1)S(1)} %bitcast.47) | data formatting | bytes 3670016
  (21 shorter events, 1.2 us)
Async XLA Ops:
  7.2 15.6 %copy-start.4 = (f32[12,7168]{1,0:T(8,128)S(1)}, f32[12,7168]{1,0:T(8,128)}, u32[]{:S(2)}) copy-start(f32[12,7168]{1,0:T(8,128)} %param.9) | copy-start | bytes 1032196
  7.2 177.8 %all-gather.2.cloned.1.call-start = ((), (), s32[]{:S(2)}) async-start(), calls=%async_computation.7 | async-start | bytes 12779520 | tf_op jit(solution)/shard_map/all_gather | solution.py:26
  10.2 32.2 %copy-start = (bf16[128,7168]{1,0:T(8,128)(2,1)S(1)}, bf16[128,7168]{1,0:T(8,128)(2,1)}, u32[]{:S(2)}) copy-start(bf16[128,7168]{1,0:T(8,128)(2,1)} %param.5) | copy-start | bytes 5505028
  10.2 27.6 %all-to-all-start.1 = ((f32[12,64,112]{2,0,1:T(8,128)}), f32[12,64,112]{2,0,1:T(8,128)S(1)}, u32[]{:S(2)}, u32[]{:S(2)}) async-start(f32[12,64,112]{2,0,1:T(8,128)} %copy.28), calls=%async_computation.1 | async-start | bytes 1048576 | tf_op jit(solution)/shard_map/all_to_all | solution.py:28
  37.8 19.1 %all-to-all-start.3 = ((f32[12,64,112]{2,0,1:T(8,128)}), f32[12,64,112]{2,0,1:T(8,128)S(1)}, u32[]{:S(2)}, u32[]{:S(2)}) async-start(f32[12,64,112]{2,0,1:T(8,128)} %copy.32), calls=%async_computation.3 | async-start | bytes 1048576 | tf_op jit(solution)/shard_map/all_to_all | solution.py:29
  56.9 34.9 %all-to-all-start.2 = ((bf16[128,64,112]{0,2,1:T(8,128)(2,1)}), bf16[128,64,112]{0,2,1:T(8,128)(2,1)S(1)}, u32[]{:S(2)}, u32[]{:S(2)}) async-start(bf16[128,64,112]{0,2,1:T(8,128)(2,1)} %bitcast.48), calls=%async_computation.2 | async-start | bytes 3670016 | tf_op jit(solution)/shard_map/all_to_all | solution.py:23
  91.7 101.5 %all-to-all-start = ((bf16[128,64,112]{0,2,1:T(8,128)(2,1)}), bf16[128,64,112]{0,2,1:T(8,128)(2,1)}, u32[]{:S(2)}, u32[]{:S(2)}) async-start(bf16[128,64,112]{0,2,1:T(8,128)(2,1)} %bitcast.46), calls=%async_computation | async-start | bytes 3670016 | tf_op jit(solution)/shard_map/all_to_all | solution.py:24
  184.7 1.0 copy-start.3
  193.2 20.5 %all-to-all-start.5 = ((f32[64,12,112]{2,1,0:T(8,128)}), f32[64,12,112]{2,1,0:T(8,128)S(1)}, u32[]{:S(2)}, u32[]{:S(2)}) async-start(f32[64,12,112]{2,1,0:T(8,128)} %all_to_all.100), calls=%async_computation.5 | async-start | bytes 1048576 | tf_op jit(solution)/shard_map/all_to_all | solution.py:38
  213.7 18.6 %all-to-all-start.6 = ((f32[64,12,112]{2,1,0:T(8,128)}), f32[64,12,112]{2,1,0:T(8,128)S(1)}, u32[]{:S(2)}, u32[]{:S(2)}) async-start(f32[64,12,112]{2,1,0:T(8,128)} %all_to_all.104), calls=%async_computation.6 | async-start | bytes 1048576 | tf_op jit(solution)/shard_map/all_to_all | solution.py:39
  232.3 0.8 copy-start.1
  233.1 34.8 %all-to-all-start.4 = ((bf16[64,128,112]{1,2,0:T(8,128)(2,1)}), bf16[64,128,112]{1,2,0:T(8,128)(2,1)S(1)}, u32[]{:S(2)}, u32[]{:S(2)}) async-start(bf16[64,128,112]{1,2,0:T(8,128)(2,1)} %bitcast.45), calls=%async_computation.4 | async-start | bytes 3670016 | tf_op jit(solution)/shard_map/all_to_all | solution.py:41
  240.2 1.2 copy-start.2
Sparse Core Ops, SparseCore 0:
  11.3 128.0 all-gather.1
where the time goes:
time: 279 us; the launch traced here: 278 us
  waiting for transfers between devices  94.6 us (34%)
  blocking collectives  79.7 us (29%)
  starting transfers between devices  48.4 us (17%)
  local copies, waits for them, and re-layouts  21.2 us (8%)
  matrix products  15.6 us (6%)
  between operations  14.9 us (5%)
  other arithmetic  3.14 us (1%)
    psum x1, blocking collectives, shards(): squares = lax.psum(jnp.sum(wide * wide), ('fsdp', 'mat'))  79.7 us
    all_to_all x1, waiting for transfers between devices, shards(): lax.all_to_all(gradient, 'fsdp', split_axis=1, concat_axis=0, tiled=True)  26.3 us
    all_to_all x1, waiting for transfers between devices, shards(): lax.all_to_all(weight_next, 'fsdp', split_axis=0, concat_axis=1, tiled=True)  25.4 us
    all_to_all x1, waiting for transfers between devices, shards(): lax.all_to_all(first_moment, 'fsdp', split_axis=1, concat_axis=0, tiled=T...  13.7 us
    all_to_all x1, waiting for transfers between devices, shards(): lax.all_to_all(first_next, 'fsdp', split_axis=0, concat_axis=1, tiled=True)  12.9 us
    all_to_all x1, starting transfers between devices, shards(): lax.all_to_all(first_moment, 'fsdp', split_axis=1, concat_axis=0, tiled=T...  12.6 us
    all_to_all x1, waiting for transfers between devices, shards(): lax.all_to_all(second_moment, 'fsdp', split_axis=1, concat_axis=0, tiled=...  12.2 us
    unnamed x13, local copies, waits for them, and re-layouts  10.6 us
  transfers between devices with their start and end apart: 8, of which 6 were waited for; matrix products, arithmetic and copies ran while one was open for 11% of the time, Pallas kernels for 0%

commit v1 on v0

v1 whole, which is shorter than its diff:
```python
import functools

import jax
import jax.numpy as jnp
from jax import lax
from jax.experimental import pallas as pl
from jax.experimental.pallas import tpu as pltpu
from jax.sharding import PartitionSpec as P

D = 8192
FW = 14336
R = 768
ROWS = 128
COLS = 7168
HALF = COLS // 2
OWN = HALF // 4
MR = 12
CHUNKS = ((0, 512), (512, 384))
K = len(CHUNKS)
MESH = pl.DeviceIdType.MESH
BF = jnp.bfloat16
F32 = jnp.float32
NT = (((1,), (1,)), ((), ()))


def kernel(
    g_ref, w_ref, p_ref, m1_ref, m2_ref,
    nw_ref, n1_ref, n2_ref,
    gl, wl, pl_, g_all, pt, pn, own, cs, cr, zs, zr, fin, ys, yr, mi, mo, df, dr, us, ur, sq, sqr,
    lsem, msem, osem,
    g_s, g_r, p_s, p_r, mi_s, mi_r, c_s, c_r, z_s, z_r, y_s, y_r,
    dy_s, dy_r, dz_s, dz_r, dc_s, dc_r, mo_s, mo_r, u_s, u_r, q_s, q_r,
):
    f = lax.axis_index("fsdp")
    yl = lax.axis_index("mat")
    c = lax.rem(f, 2)
    yh = lax.rem(lax.div(f, 2), 2)
    z = lax.rem(lax.div(f, 4), 4)
    x = lax.div(f, 16)

    def dev(x_, z_, yh_, yl_, c_):
        return (((x_ * 4 + z_) * 2 + yh_) * 2 + c_, yl_)

    def along_x(d):
        return dev(lax.rem(x + d, 4), z, yh, yl, c)

    def along_z(d):
        return dev(x, lax.rem(z + d, 4), yh, yl, c)

    def along_y(d):
        t = lax.rem(yh * 2 + yl + d, 4)
        return dev(x, z, lax.div(t, 2), lax.rem(t, 2), c)

    mate = dev(x, z, yh, yl, 1 - c)
    across = dev(x, z, 1 - yh, yl, c)
    grp = (along_x, along_z)
    red = (along_z, along_x)
    gq = (x, z)
    rq = (z, x)

    def rows(start, size, of):
        return pl.ds(pl.multiple_of(start, of), size)

    def at_cols(h, j, k):
        return rows(h * HALF + j * OWN + CHUNKS[k][0], CHUNKS[k][1], 128)

    def remote(src, dst, s, r, to):
        return pltpu.make_async_remote_copy(
            src_ref=src, dst_ref=dst, send_sem=s, recv_sem=r, device_id=to, device_id_type=MESH
        )

    load_p = pltpu.make_async_copy(p_ref, pl_, lsem.at[0])
    load_g = pltpu.make_async_copy(g_ref, gl, lsem.at[1])
    load_w = pltpu.make_async_copy(w_ref, wl, lsem.at[2])
    load_p.start()
    load_g.start()
    load_w.start()

    barrier = pltpu.get_barrier_semaphore()
    partners = [mate] + [a(d) for a in (along_x, along_z, along_y) for d in (1, 2, 3)]
    for to in partners:
        pl.semaphore_signal(barrier, inc=1, device_id=to, device_id_type=MESH)

    load_p.wait()
    for h in range(2):
        for b in range(R // 128):
            i = lax.broadcasted_iota(jnp.int32, (128, 128), 0) + b * 128
            t = lax.rem(i, MR)
            i = lax.div(i, MR)
            j = lax.rem(i, 4)
            i = lax.div(i, 4)
            yh_ = lax.rem(i, 2)
            i = lax.div(i, 2)
            r_ = lax.rem(i, 4)
            c_ = lax.div(i, 4)
            x_, z_ = (j, r_) if h == 0 else (r_, j)
            want = (((x_ * 4 + z_) * 2 + yh_) * 2 + c_) * MR + t
            lane = lax.broadcasted_iota(jnp.int32, (128, 128), 1)
            one = jnp.concatenate(
                [jnp.where(want == lane + n * 128, 1.0, 0.0).astype(BF) for n in range(R // 128)], axis=1
            )
            pt[h, b * 128 : (b + 1) * 128, rows(gq[h] * ROWS, ROWS, ROWS)] = lax.dot_general(
                one, pl_[...], NT, preferred_element_type=F32
            ).astype(BF)

    pl.semaphore_wait(barrier, len(partners))

    def p_copy(h, d):
        mine = pt.at[h, :, rows(gq[h] * ROWS, ROWS, ROWS)]
        return remote(mine, mine, p_s.at[h, d - 1], p_r.at[h, d - 1], grp[h](d))

    def g_copy(h, k, d):
        j = lax.rem(gq[h] + d, 4)
        off, n = CHUNKS[k]
        return remote(
            g_ref.at[:, at_cols(h, j, k)],
            g_all.at[h, rows(gq[h] * ROWS, ROWS, ROWS), pl.ds(off, n)],
            g_s.at[h, k, d - 1], g_r.at[h, k, d - 1], grp[h](d),
        )

    def g_own(h):
        return pltpu.make_async_copy(
            g_ref.at[:, rows(h * HALF + gq[h] * OWN, OWN, 128)],
            g_all.at[h, rows(gq[h] * ROWS, ROWS, ROWS), :],
            lsem.at[3 + h],
        )

    def mi_copy(h, m, d):
        j = lax.rem(gq[h] + d, 4)
        return remote(
            (m1_ref, m2_ref)[m].at[:, rows(h * HALF + j * OWN, OWN, 128)],
            mi.at[h, m, gq[h]],
            mi_s.at[h, m, d - 1], mi_r.at[h, m, d - 1], grp[h](d),
        )

    def mi_own(h, m):
        return pltpu.make_async_copy(
            (m1_ref, m2_ref)[m].at[:, rows(h * HALF + gq[h] * OWN, OWN, 128)], mi.at[h, m, gq[h]], msem.at[h, m]
        )

    order = (2, 1, 3)
    for d in order:
        for h in range(2):
            p_copy(h, d).start()
    for k in range(K):
        for d in order:
            for h in range(2):
                g_copy(h, k, d).start()
    for h in range(2):
        g_own(h).start()
        for m in range(2):
            mi_own(h, m).start()
    for d in order:
        for h in range(2):
            for m in range(2):
                mi_copy(h, m, d).start()

    load_g.wait()

    def add_squares(i, total):
        block = gl[rows(i * 16, 16, 16), :].astype(F32)
        block = block * block
        for n in range(COLS // 1024):
            part = block[:, n * 1024 : (n + 1) * 1024]
            total = total + part
        return total

    total = lax.fori_loop(0, ROWS // 16, add_squares, jnp.zeros((16, 1024), F32))
    total = total[:8] + total[8:]
    part = total[:, :128]
    for n in range(1, 8):
        part = part + total[:, n * 128 : (n + 1) * 128]
    at = 0
    for stage, to in enumerate(([mate], *([a(d) for d in (1, 2, 3)] for a in (along_x, along_z, along_y)))):
        sq[stage] = part
        copies = [
            remote(sq.at[stage], sqr.at[at + n], q_s.at[at + n], q_r.at[at + n], who) for n, who in enumerate(to)
        ]
        for copy in copies:
            copy.start()
        for copy in copies:
            copy.wait()
        for n in range(len(to)):
            part = part + sqr[at + n]
        at += len(to)
    squares = jnp.sum(jnp.sum(part, axis=1, keepdims=True), axis=0, keepdims=True)
    clip = jnp.minimum(1.0, 1.0 / jnp.sqrt(squares / (D * FW) + 1e-06))

    def c_copy(h, k):
        cols = pl.ds(*CHUNKS[k])
        return remote(cs.at[h, :, cols], cr.at[h, :, cols], c_s.at[h, k], c_r.at[h, k], mate)

    def z_copy(h, k, d):
        cols = pl.ds(*CHUNKS[k])
        to = lax.rem(rq[h] + d, 4)
        return remote(
            zs.at[h, rows(to * 96, 96, 96), cols], zr.at[h, d - 1, :, cols],
            z_s.at[h, k, d - 1], z_r.at[h, k, d - 1], red[h](d),
        )

    def y_copy(h, k):
        cols = pl.ds(*CHUNKS[k])
        return remote(ys.at[h, :, cols], yr.at[h, :, cols], y_s.at[h, k], y_r.at[h, k], across)

    def dr_rows(h, yh_):
        return rows(c * 384 + rq[h] * 96 + yh_ * 48, 48, 48)

    def dy_copy(h, k):
        mine = dr.at[h, dr_rows(h, yh), pl.ds(*CHUNKS[k])]
        return remote(mine, mine, dy_s.at[h, k], dy_r.at[h, k], across)

    def dz_copy(h, k, e, d):
        mine = dr.at[h, dr_rows(h, yh if e == 0 else 1 - yh), pl.ds(*CHUNKS[k])]
        return remote(mine, mine, dz_s.at[h, k, e, d - 1], dz_r.at[h, k, e, d - 1], red[h](d))

    def dc_copy(h, k):
        mine = dr.at[h, rows(c * 384, 384, 384), pl.ds(*CHUNKS[k])]
        return remote(mine, mine, dc_s.at[h, k], dc_r.at[h, k], mate)

    def mo_copy(h, k, m, d):
        j = lax.rem(gq[h] + d, 4)
        return remote(
            mo.at[h, m, j, :, pl.ds(*CHUNKS[k])], (n1_ref, n2_ref)[m].at[:, at_cols(h, gq[h], k)],
            mo_s.at[h, k, m, d - 1], mo_r.at[h, k, m, d - 1], grp[h](d),
        )

    def mo_own(h, k, m):
        return pltpu.make_async_copy(
            mo.at[h, m, gq[h], :, pl.ds(*CHUNKS[k])], (n1_ref, n2_ref)[m].at[:, at_cols(h, gq[h], k)],
            osem.at[h, k, m],
        )

    def u_copy(h, k, d):
        j = lax.rem(gq[h] + d, 4)
        return remote(
            us.at[h, rows(j * ROWS, ROWS, ROWS), pl.ds(*CHUNKS[k])], ur.at[:, at_cols(h, gq[h], k)],
            u_s.at[h, k, d - 1], u_r.at[h, k, d - 1], grp[h](d),
        )

    def nw_copy(h, k, j):
        return pltpu.make_async_copy(
            wl.at[:, at_cols(h, j, k)], nw_ref.at[:, at_cols(h, j, k)], osem.at[h, k, 2]
        )

    def multiply(k):
        off, n = CHUNKS[k]
        cols = slice(off, off + n)
        for h in range(2):
            if k == 0:
                g_own(h).wait()
                for d in order:
                    p_copy(h, d).wait()
            for d in order:
                g_copy(h, k, d).wait()
            for b in range(3):
                cs[h, b * 128 : (b + 1) * 128, cols] = jnp.dot(
                    pt[h, rows((1 - c) * 384 + b * 128, 128, 128), :], g_all[h, :, cols], preferred_element_type=F32
                ).astype(BF)
            c_copy(h, k).start()
        for h in range(2):
            for b in range(3):
                own[h, b * 128 : (b + 1) * 128, cols] = jnp.dot(
                    pt[h, rows(c * 384 + b * 128, 128, 128), :], g_all[h, :, cols], preferred_element_type=F32
                )

    def add_core(k):
        off, n = CHUNKS[k]
        cols = slice(off, off + n)
        for h in range(2):
            c_copy(h, k).wait()
            for d in order:
                part = rows(lax.rem(rq[h] + d, 4) * 96, 96, 96)
                zs[h, part, cols] = (own[h, part, cols] + cr[h, part, cols].astype(F32)).astype(BF)
                z_copy(h, k, d).start()

    def add_ring(k):
        off, n = CHUNKS[k]
        cols = slice(off, off + n)
        for h in range(2):
            for d in order:
                z_copy(h, k, d).wait()

            def total(yh_):
                part = rows(rq[h] * 96 + yh_ * 48, 48, 48)
                sum_ = own[h, part, cols] + cr[h, part, cols].astype(F32)
                for e in range(3):
                    sum_ = sum_ + zr[h, e, rows(yh_ * 48, 48, 48), cols].astype(F32)
                return sum_

            ys[h, :, cols] = total(1 - yh).astype(BF)
            y_copy(h, k).start()
            fin[h, :, cols] = total(yh)

    def adam(k):
        off, n = CHUNKS[k]
        cols = slice(off, off + n)
        for h in range(2):
            if k == 0:
                for m in range(2):
                    mi_own(h, m).wait()
                    for d in order:
                        mi_copy(h, m, d).wait()
            y_copy(h, k).wait()
            fin[h, :, cols] = fin[h, :, cols] + yr[h, :, cols].astype(F32)
            for j in range(4):
                scaled = clip * fin[h, j * MR : (j + 1) * MR, cols]
                first = 0.9 * mi[h, 0, j, :, cols] + 0.1 * scaled
                second = 0.95 * mi[h, 1, j, :, cols] + 0.05 * scaled * scaled
                mo[h, 0, j, :, cols] = first
                mo[h, 1, j, :, cols] = second
                df[h, j * MR : (j + 1) * MR, cols] = first / (jnp.sqrt(second) + 1e-08)
            dr[h, dr_rows(h, yh), cols] = df[h, :, cols].astype(BF)
            dy_copy(h, k).start()
            for d in order:
                dz_copy(h, k, 0, d).start()
        for h in range(2):
            for m in range(2):
                mo_own(h, k, m).start()
                for d in order:
                    mo_copy(h, k, m, d).start()

    def spread(k):
        for h in range(2):
            dy_copy(h, k).wait()
            for d in order:
                dz_copy(h, k, 1, d).start()

    def share(k):
        for h in range(2):
            for e in range(2):
                for d in order:
                    dz_copy(h, k, e, d).wait()
            dc_copy(h, k).start()

    def transpose_projector():
        for h in range(2):
            for b in range(R // 128):
                i = lax.broadcasted_iota(jnp.int32, (512, 512), 0)
                eye = (i == lax.broadcasted_iota(jnp.int32, (512, 512), 1)).astype(F32).astype(BF)
                pn[h, :, b * 128 : (b + 1) * 128] = lax.dot_general(
                    eye, pt[h, b * 128 : (b + 1) * 128, :], NT, preferred_element_type=F32
                ).astype(BF)

    def update(k):
        off, n = CHUNKS[k]
        cols = slice(off, off + n)
        for h in range(2):
            dc_copy(h, k).wait()
            for d in (2, 1, 3, 0):
                part = rows(lax.rem(gq[h] + d, 4) * ROWS, ROWS, ROWS)
                us[h, part, cols] = jnp.dot(pn[h, part, :], dr[h, :, cols], preferred_element_type=F32).astype(BF)
                if d:
                    u_copy(h, k, d).start()

    def weight(k):
        off, n = CHUNKS[k]
        cols = slice(off, off + n)
        for h in range(2):
            for d in (0, 1, 3, 2):
                j = lax.rem(gq[h] - d + 4, 4)
                here = at_cols(h, j, k)
                if d:
                    u_copy(h, k, d).wait()
                    u = ur[:, here]
                else:
                    u = us[h, rows(gq[h] * ROWS, ROWS, ROWS), cols]
                wl[:, here] = (wl[:, here].astype(F32) - 0.25 * u.astype(F32)).astype(BF)

    last = K + 7
    for step in range(last):
        for s, run in reversed(list(enumerate((multiply, add_core, add_ring, adam, spread, share, update)))):
            if 0 <= step - s < K:
                run(step - s)
        if step == 1:
            transpose_projector()
    load_w.wait()
    for k in range(K):
        weight(k)
    out = pltpu.make_async_copy(wl, nw_ref, lsem.at[5])
    out.start()
    for k in range(K):
        for h in range(2):
            for m in range(2):
                mo_own(h, k, m).wait()
                for d in order:
                    mo_copy(h, k, m, d).wait()
    out.wait()


def shards(gradient, weight, projector, first_moment, second_moment):
    dma = pltpu.SemaphoreType.DMA
    hk = dma((2, K))
    hkd = dma((2, K, 3))
    return pl.pallas_call(
        kernel,
        out_shape=(
            jax.ShapeDtypeStruct((ROWS, COLS), BF),
            jax.ShapeDtypeStruct((MR, COLS), F32),
            jax.ShapeDtypeStruct((MR, COLS), F32),
        ),
        in_specs=[pl.BlockSpec(memory_space=pl.ANY)] * 5,
        out_specs=[pl.BlockSpec(memory_space=pl.ANY)] * 3,
        scratch_shapes=[
            pltpu.VMEM((ROWS, COLS), BF),
            pltpu.VMEM((ROWS, COLS), BF),
            pltpu.VMEM((ROWS, R), BF),
            pltpu.VMEM((2, 512, OWN), BF),
            pltpu.VMEM((2, R, 512), BF),
            pltpu.VMEM((2, 512, R), BF),
            pltpu.VMEM((2, 384, OWN), F32),
            pltpu.VMEM((2, 384, OWN), BF),
            pltpu.VMEM((2, 384, OWN), BF),
            pltpu.VMEM((2, 384, OWN), BF),
            pltpu.VMEM((2, 3, 96, OWN), BF),
            pltpu.VMEM((2, 48, OWN), F32),
            pltpu.VMEM((2, 48, OWN), BF),
            pltpu.VMEM((2, 48, OWN), BF),
            pltpu.VMEM((2, 2, 4, MR, OWN), F32),
            pltpu.VMEM((2, 2, 4, MR, OWN), F32),
            pltpu.VMEM((2, 48, OWN), F32),
            pltpu.VMEM((2, R, OWN), BF),
            pltpu.VMEM((2, 512, OWN), BF),
            pltpu.VMEM((ROWS, COLS), BF),
            pltpu.VMEM((4, 8, 128), F32),
            pltpu.VMEM((10, 8, 128), F32),
            dma((6,)), dma((2, 2)), dma((2, K, 3)),
            hkd, hkd,
            dma((2, 3)), dma((2, 3)),
            dma((2, 2, 3)), dma((2, 2, 3)),
            hk, hk,
            hkd, hkd,
            hk, hk,
            hk, hk,
            dma((2, K, 2, 3)), dma((2, K, 2, 3)),
            hk, hk,
            dma((2, K, 2, 3)), dma((2, K, 2, 3)),
            hkd, hkd,
            dma((10,)), dma((10,)),
        ],
        compiler_params=pltpu.CompilerParams(
            collective_id=0, has_side_effects=True, vmem_limit_bytes=50 * 1024 * 1024
        ),
        cost_estimate=pl.CostEstimate(flops=4 * ROWS * R * COLS, bytes_accessed=7_000_000, transcendentals=86016),
    )(gradient, weight, projector, first_moment, second_moment)


def solution(mesh):
    split = P("fsdp", "mat")
    return jax.shard_map(
        shards,
        mesh=mesh,
        in_specs=(split, split, P("fsdp", None), split, split),
        out_specs=(split, split, split),
        check_vma=False,
    )
```

time: 279 us -> 88.6 us (0.32)
  waiting for transfers between devices: 94.6 us -> 0 us
  Pallas kernels: 0 us -> 82 us
  blocking collectives: 79.7 us -> 0 us
  starting transfers between devices: 48.4 us -> 0 us
  matrix products: 15.6 us -> 0 us
  local copies, waits for them, and re-layouts: 21.2 us -> 5.72 us
  between operations: 14.9 us -> 0.65 us
  other arithmetic: 3.14 us -> 0 us
    all_to_all x7 -> x0, waiting for transfers between devices: 93.9 us -> none  [the longest x1 26.3 us: shards(): lax.all_to_all(gradient, 'fsdp', split_axis=1, concat_axis=0, tiled=True)]
    pallas_call x0 -> x1, Pallas kernels: none -> 82 us  [shards(): pl.pallas_call(kernel, out_shape=(jax.ShapeDtypeStruct((ROWS, COLS), BF),...]
    psum x1 -> x0, blocking collectives: 79.7 us -> none  [shards(): squares = lax.psum(jnp.sum(wide * wide), ('fsdp', 'mat'))]
    all_to_all x7 -> x0, starting transfers between devices: 48.4 us -> none  [the longest x1 12.6 us: shards(): lax.all_to_all(first_moment, 'fsdp', split_axis=1, concat_axis=0, tiled=T...]
    dot_general x2 -> x0, matrix products: 15.6 us -> none  [the longest x1 9.11 us: shards(): jnp.dot(whole_projector, direction, preferred_element_type=jnp.float32)]
    all_to_all x11 -> x0, local copies, waits for them, and re-layouts: 9.16 us -> none  [the longest x2 2.27 us: shards(): lax.all_to_all(first_moment, 'fsdp', split_axis=1, concat_axis=0, tiled=T...]
    unnamed x13 -> x9, local copies, waits for them, and re-layouts: 10.6 us -> 5.72 us
    reduce_sum x1 -> x0, other arithmetic: 3.05 us -> none  [shards(): squares = lax.psum(jnp.sum(wide * wide), ('fsdp', 'mat'))]
  transfers between devices with their start and end apart: 8 -> 0, of which waited for: 6 -> 0; matrix products, arithmetic and copies ran while one was open for 11% -> 0% of each run, Pallas kernels for 0% -> 0%
where the time goes in v1:
time: 88.6 us; the launch traced here: 88.4 us
  Pallas kernels  82 us (93%)
  local copies, waits for them, and re-layouts  5.72 us (6%)
    pallas_call x1, Pallas kernels, shards(): pl.pallas_call(kernel, out_shape=(jax.ShapeDtypeStruct((ROWS, COLS), BF),...  82 us
    unnamed x9, local copies, waits for them, and re-layouts  5.72 us

profile of v1, /device:TPU:1, one launch (start us, length us, event | category | flops | bytes accessed | tf_op | source)
XLA Modules:
  0.0 88.4 jit_solution(7503379328848680094)
XLA Ops:
  0.6 0.0 copy-start
  0.6 1.0 %copy-done = f32[12,7168]{1,0:T(8,128)S(1)} copy-done((f32[12,7168]{1,0:T(8,128)S(1)}, f32[12,7168]{1,0:T(8,128)}, u32[]{:S(2)}) %copy-start) | copy-done | bytes 344088
  1.7 0.0 copy-start.1
  1.7 1.0 %copy-done.1 = f32[12,7168]{1,0:T(8,128)S(1)} copy-done((f32[12,7168]{1,0:T(8,128)S(1)}, f32[12,7168]{1,0:T(8,128)}, u32[]{:S(2)}) %copy-start.1) | copy-done | bytes 344088
  2.7 0.0 copy-start.2
  2.7 0.9 %copy-done.2 = bf16[128,768]{1,0:T(8,128)(2,1)S(1)} copy-done((bf16[128,768]{1,0:T(8,128)(2,1)S(1)}, bf16[128,768]{1,0:T(8,128)(2,1)}, u32[]{:S(2)}) %copy-start.2) | copy-done | bytes 196632
  3.6 82.0 %shard_map.76 = (bf16[128,7168]{1,0:T(8,128)(2,1)S(1)}, f32[12,7168]{1,0:T(8,128)S(1)}, f32[12,7168]{1,0:T(8,128)S(1)}) custom-call(bf16[128,7168]{1,0:T(8,128)(2,1)} %g_ref.1, bf16[128,7168]{1,0:T(8,128)(2,1)} %w_ref.1, bf16[128,768]{1,0:T(8,128)(2,1)S(1)} %copy-done.2, f32[12,7168]{1,0:T(8,128)S(1)} %copy-done, f32[12,7168]{1,0:T(8,128)S(1)} %copy-done.1), custom_call_target="tpu_custom_call" | custom-call | flops 2818572288 | bytes 7000000 | tf_op jit(solution)/shard_map/pallas_call | solution.py:394
  85.6 1.2 %copy.11 = bf16[128,7168]{1,0:T(8,128)(2,1)} copy(bf16[128,7168]{1,0:T(8,128)(2,1)S(1)} %get-tuple-element.6) | data formatting | bytes 3670016
  86.9 0.8 copy.12
  87.6 0.8 copy.13
Async XLA Ops:
  0.6 1.0 %copy-start = (f32[12,7168]{1,0:T(8,128)S(1)}, f32[12,7168]{1,0:T(8,128)}, u32[]{:S(2)}) copy-start(f32[12,7168]{1,0:T(8,128)} %m1_ref.1) | copy-start | bytes 1032196
  1.7 1.0 %copy-start.1 = (f32[12,7168]{1,0:T(8,128)S(1)}, f32[12,7168]{1,0:T(8,128)}, u32[]{:S(2)}) copy-start(f32[12,7168]{1,0:T(8,128)} %m2_ref.1) | copy-start | bytes 1032196
  2.7 0.9 %copy-start.2 = (bf16[128,768]{1,0:T(8,128)(2,1)S(1)}, bf16[128,768]{1,0:T(8,128)(2,1)}, u32[]{:S(2)}) copy-start(bf16[128,768]{1,0:T(8,128)(2,1)} %p_ref.1) | copy-start | bytes 589828

commit v2 on v1

--- a/solution.py
+++ b/solution.py
@@ -26,7 +26,7 @@
 def kernel(
     g_ref, w_ref, p_ref, m1_ref, m2_ref,
     nw_ref, n1_ref, n2_ref,
-    gl, wl, pl_, g_all, pt, pn, own, cs, cr, zs, zr, fin, ys, yr, mi, mo, df, dr, us, ur, sq, sqr,
+    gl, wl, pl_, g_all, pt, pn, own, cs, cr, zs, zr, fin, ys, yr, mi, mo, df, dr, us, ur, sq, sqr, scale,
     lsem, msem, osem,
     g_s, g_r, p_s, p_r, mi_s, mi_r, c_s, c_r, z_s, z_r, y_s, y_r,
     dy_s, dy_r, dz_s, dz_r, dc_s, dc_r, mo_s, mo_r, u_s, u_r, q_s, q_r,
@@ -150,11 +150,6 @@
         g_own(h).start()
         for m in range(2):
             mi_own(h, m).start()
-    for d in order:
-        for h in range(2):
-            for m in range(2):
-                mi_copy(h, m, d).start()
-
     load_g.wait()
 
     def add_squares(i, total):
@@ -170,21 +165,36 @@
     part = total[:, :128]
     for n in range(1, 8):
         part = part + total[:, n * 128 : (n + 1) * 128]
-    at = 0
-    for stage, to in enumerate(([mate], *([a(d) for d in (1, 2, 3)] for a in (along_x, along_z, along_y)))):
-        sq[stage] = part
-        copies = [
-            remote(sq.at[stage], sqr.at[at + n], q_s.at[at + n], q_r.at[at + n], who) for n, who in enumerate(to)
-        ]
-        for copy in copies:
+    def sq_copies(stage):
+        to = ([mate], *([a(d) for d in (1, 2, 3)] for a in (along_y, along_x, along_z)))[stage]
+        at = (0, 1, 4, 7)[stage]
+        return [remote(sq.at[stage], sqr.at[at + n], q_s.at[at + n], q_r.at[at + n], who) for n, who in enumerate(to)]
+
+    def sq_start(stage):
+        for copy in sq_copies(stage):
             copy.start()
+
+    def sq_done(stage):
+        copies = sq_copies(stage)
+        at = (0, 1, 4, 7)[stage]
         for copy in copies:
             copy.wait()
-        for n in range(len(to)):
+        part = sq[stage]
+        for n in range(len(copies)):
             part = part + sqr[at + n]
-        at += len(to)
-    squares = jnp.sum(jnp.sum(part, axis=1, keepdims=True), axis=0, keepdims=True)
-    clip = jnp.minimum(1.0, 1.0 / jnp.sqrt(squares / (D * FW) + 1e-06))
+        if stage < 3:
+            sq[stage + 1] = part
+            sq_start(stage + 1)
+        return part
+
+    sq[0] = part
+    sq_start(0)
+    sq_done(0)
+    sq_done(1)
+
+    def clip_of(part):
+        squares = jnp.sum(jnp.sum(part, axis=1, keepdims=True), axis=0, keepdims=True)
+        return jnp.minimum(1.0, 1.0 / jnp.sqrt(squares / (D * FW) + 1e-06))
 
     def c_copy(h, k):
         cols = pl.ds(*CHUNKS[k])
@@ -237,11 +247,6 @@
             u_s.at[h, k, d - 1], u_r.at[h, k, d - 1], grp[h](d),
         )
 
-    def nw_copy(h, k, j):
-        return pltpu.make_async_copy(
-            wl.at[:, at_cols(h, j, k)], nw_ref.at[:, at_cols(h, j, k)], osem.at[h, k, 2]
-        )
-
     def multiply(k):
         off, n = CHUNKS[k]
         cols = slice(off, off + n)
@@ -272,10 +277,17 @@
                 part = rows(lax.rem(rq[h] + d, 4) * 96, 96, 96)
                 zs[h, part, cols] = (own[h, part, cols] + cr[h, part, cols].astype(F32)).astype(BF)
                 z_copy(h, k, d).start()
+        if k == 0:
+            for d in order:
+                for h in range(2):
+                    for m in range(2):
+                        mi_copy(h, m, d).start()
 
     def add_ring(k):
         off, n = CHUNKS[k]
         cols = slice(off, off + n)
+        if k == 0:
+            sq_done(2)
         for h in range(2):
             for d in order:
                 z_copy(h, k, d).wait()
@@ -294,6 +306,9 @@
     def adam(k):
         off, n = CHUNKS[k]
         cols = slice(off, off + n)
+        if k == 0:
+            scale[...] = jnp.broadcast_to(clip_of(sq_done(3)), (8, 128))
+        clip = scale[:1, :1]
         for h in range(2):
             if k == 0:
                 for m in range(2):
@@ -364,7 +379,7 @@
                     u = ur[:, here]
                 else:
                     u = us[h, rows(gq[h] * ROWS, ROWS, ROWS), cols]
-                wl[:, here] = (wl[:, here].astype(F32) - 0.25 * u.astype(F32)).astype(BF)
+                nw_ref[:, here] = (wl[:, here].astype(F32) - 0.25 * u.astype(F32)).astype(BF)
 
     last = K + 7
     for step in range(last):
@@ -376,30 +391,28 @@
     load_w.wait()
     for k in range(K):
         weight(k)
-    out = pltpu.make_async_copy(wl, nw_ref, lsem.at[5])
-    out.start()
     for k in range(K):
         for h in range(2):
             for m in range(2):
                 mo_own(h, k, m).wait()
                 for d in order:
                     mo_copy(h, k, m, d).wait()
-    out.wait()
-
-
-def shards(gradient, weight, projector, first_moment, second_moment):
+
+
+def shards(*inputs):
+    inputs = [pltpu.with_memory_space_constraint(a, pltpu.HBM) for a in inputs]
     dma = pltpu.SemaphoreType.DMA
     hk = dma((2, K))
     hkd = dma((2, K, 3))
     return pl.pallas_call(
         kernel,
         out_shape=(
-            jax.ShapeDtypeStruct((ROWS, COLS), BF),
-            jax.ShapeDtypeStruct((MR, COLS), F32),
-            jax.ShapeDtypeStruct((MR, COLS), F32),
+            pltpu.VMEM((ROWS, COLS), BF),
+            pltpu.VMEM((MR, COLS), F32),
+            pltpu.VMEM((MR, COLS), F32),
         ),
         in_specs=[pl.BlockSpec(memory_space=pl.ANY)] * 5,
-        out_specs=[pl.BlockSpec(memory_space=pl.ANY)] * 3,
+        out_specs=[pl.BlockSpec(memory_space=pltpu.VMEM)] * 3,
         scratch_shapes=[
             pltpu.VMEM((ROWS, COLS), BF),
             pltpu.VMEM((ROWS, COLS), BF),
@@ -423,6 +436,7 @@
             pltpu.VMEM((ROWS, COLS), BF),
             pltpu.VMEM((4, 8, 128), F32),
             pltpu.VMEM((10, 8, 128), F32),
+            pltpu.VMEM((8, 128), F32),
             dma((6,)), dma((2, 2)), dma((2, K, 3)),
             hkd, hkd,
             dma((2, 3)), dma((2, 3)),
@@ -441,7 +455,7 @@
             collective_id=0, has_side_effects=True, vmem_limit_bytes=50 * 1024 * 1024
         ),
         cost_estimate=pl.CostEstimate(flops=4 * ROWS * R * COLS, bytes_accessed=7_000_000, transcendentals=86016),
-    )(gradient, weight, projector, first_moment, second_moment)
+    )(*inputs)
 
 
 def solution(mesh):

time: 88.6 us -> 71.7 us (0.81)
  Pallas kernels: 82 us -> 68.1 us
  local copies, waits for them, and re-layouts: 5.72 us -> 2.76 us
    pallas_call x1, Pallas kernels: 82 us -> 68.1 us  [shards(): pl.pallas_call(kernel, out_shape=(pltpu.VMEM((ROWS, COLS), BF), pltpu.VME...]
    unnamed x9 -> x3, local copies, waits for them, and re-layouts: 5.72 us -> 2.76 us
where the time goes in v2:
time: 71.7 us; the launch traced here: 71.5 us
  Pallas kernels  68.1 us (95%)
  local copies, waits for them, and re-layouts  2.76 us (4%)
    pallas_call x1, Pallas kernels, shards(): pl.pallas_call(kernel, out_shape=(pltpu.VMEM((ROWS, COLS), BF), pltpu.VME...  68.1 us
    unnamed x3, local copies, waits for them, and re-layouts  2.76 us

profile of v2, /device:TPU:1, one launch (start us, length us, event | category | flops | bytes accessed | tf_op | source)
XLA Modules:
  0.0 71.5 jit_solution(4787059193700372045)
XLA Ops:
  0.6 68.1 %shard_map.76 = (bf16[128,7168]{1,0:T(8,128)(2,1)S(1)}, f32[12,7168]{1,0:T(8,128)S(1)}, f32[12,7168]{1,0:T(8,128)S(1)}) custom-call(bf16[128,7168]{1,0:T(8,128)(2,1)} %g_ref.1, bf16[128,7168]{1,0:T(8,128)(2,1)} %w_ref.1, bf16[128,768]{1,0:T(8,128)(2,1)} %p_ref.1, f32[12,7168]{1,0:T(8,128)} %m1_ref.1, f32[12,7168]{1,0:T(8,128)} %m2_ref.1), custom_call_target="tpu_custom_call" | custom-call | flops 2818572288 | bytes 7000000 | tf_op jit(solution)/shard_map/pallas_call | solution.py:407
  68.8 1.2 %copy.11 = bf16[128,7168]{1,0:T(8,128)(2,1)} copy(bf16[128,7168]{1,0:T(8,128)(2,1)S(1)} %get-tuple-element.3) | data formatting | bytes 3670016
  70.0 0.8 %copy.12 = f32[12,7168]{1,0:T(8,128)} copy(f32[12,7168]{1,0:T(8,128)S(1)} %get-tuple-element.4) | data formatting | bytes 688128
  70.8 0.8 %copy.13 = f32[12,7168]{1,0:T(8,128)} copy(f32[12,7168]{1,0:T(8,128)S(1)} %get-tuple-element.5) | data formatting | bytes 688128
